TPU v7x, 32 devices: a whole 2x2x4 slice. The times are simulated.
32 devices in a mesh: dst: 8 (over y, x, core), src: 4 (over z).
Axes of the slice: x: 2, y: 2, z: 4, core: 2. Of those that a mesh axis runs over, the one named last changes fastest.
Arguments:
- points: bfloat16 [4096, 256], P(('dst', 'src')), may hold values from -6 to 6
- w_query: bfloat16 [256, 256], replicated, may hold values from -16 to 16
- w_key: bfloat16 [256, 256], replicated, may hold values from -0.375 to 0.375
- w_value: bfloat16 [256, 256], replicated, may hold values from -0.375 to 0.375
- w_out: bfloat16 [256, 256], replicated, may hold values from -0.375 to 0.375
- gain: float32 [256], replicated, may hold values from 0.25 to 1.75
- cell_counts: int32 [8, 4], P('dst', 'src'), may hold values from 2 to 16, as said below
- tile_slots: int32 [8, 4, 16], P('dst', 'src'), may hold values from 0 to 31, as said below
- edge_masks: int32 [8, 4, 16, 128, 128], P('dst', 'src'), may hold values 0 or 1
Outputs:
- out_points: bfloat16 [4096, 256], P(('dst', 'src'))
Inputs may be any that keep to these rules, and one draw needn't show every extreme that they name: `cell_counts`: the busiest cell lists exactly 16 tiles. `tile_slots`: within one cell the 16 tile numbers are all different.
All inputs are finite; a program needn't handle non-finite values. No bound on the sum of `edge_masks` on one device may be relied on, other than what follows from the above.
Results may differ from a plain program's by a relative error of at most 0.0085.
The roundings to bfloat16 on the way count: a program that leaves them out, or rounds other values in their place, can miss the bound.
Values may be sent and summed in bfloat16 or wider, within the bound.
A program may use at most 64 MiB of HBM per device.

v0:
```python
import math

import jax
import jax.numpy as jnp
from jax import lax
from jax.sharding import PartitionSpec as P

HEADS = 4
TILE = 128


def inverse_sinh(ratio):
    return jnp.log(ratio + jnp.sqrt(ratio * ratio + 1.0))


def log_map(points):
    values_f = points.astype(jnp.float32)
    radius = jnp.sqrt(jnp.sum(values_f * values_f, axis=-1, keepdims=True) + 1e-06)
    root_width = math.sqrt(points.shape[-1])
    return (root_width * inverse_sinh(radius / root_width) * values_f / radius).astype(jnp.bfloat16)


def exp_map(normed):
    radius = jnp.sqrt(jnp.sum(normed * normed, axis=-1, keepdims=True) + 1e-06)
    root_width = math.sqrt(normed.shape[-1])
    return (root_width * jnp.sinh(radius / root_width) * normed / radius).astype(jnp.bfloat16)


def project(rows, weight):
    return jnp.dot(rows, weight, preferred_element_type=jnp.float32).astype(jnp.bfloat16)


def head_scale(factor, head_size):
    return jnp.repeat(factor.T, head_size, axis=1)


def attend_cell(queries, key_rows, value_rows, tile_count, slot_list, mask_list):
    rows_all = queries.shape[0]
    width = queries.shape[1]
    head_size = width // HEADS
    col_tiles = key_rows.shape[0] // TILE
    score_scale = 1.0 / math.sqrt(head_size)
    q_tiles = queries.reshape(rows_all // TILE, TILE, HEADS, head_size)
    k_tiles = key_rows.reshape(col_tiles, TILE, HEADS, head_size)
    v_tiles = value_rows.reshape(col_tiles, TILE, HEADS, head_size)
    tile_group = 4
    start_state = (
        jnp.full((HEADS, rows_all), -1e30, jnp.float32),
        jnp.zeros((HEADS, rows_all), jnp.float32),
        jnp.zeros((rows_all, width), jnp.float32),
    )

    def step_group(step_index, carried):
        first_slot = step_index * tile_group
        picked = lax.dynamic_slice_in_dim(slot_list, first_slot, tile_group, 0)
        live_tiles = first_slot + jnp.arange(tile_group, dtype=jnp.int32) < tile_count
        mask_group = lax.dynamic_slice_in_dim(mask_list, first_slot, tile_group, 0)
        row_ids = picked // col_tiles
        col_ids = picked % col_tiles
        q_group = q_tiles[row_ids]
        k_group = k_tiles[col_ids]
        v_group = v_tiles[col_ids]
        scores = (
            jnp.einsum("tihe,tjhe->thij", q_group, k_group, preferred_element_type=jnp.float32)
            * score_scale
        )
        edge_live = ((mask_group == 1) & live_tiles[:, None, None])[:, None, :, :]
        masked = jnp.where(edge_live, scores, -1e30)
        tile_max = jnp.max(masked, axis=-1)
        weights = jnp.where(edge_live, jnp.exp(masked - tile_max[..., None]), 0.0)
        tile_sum = jnp.sum(weights, axis=-1)
        tile_acc = jnp.einsum(
            "thij,tjhe->tihe",
            weights.astype(jnp.bfloat16),
            v_group,
            preferred_element_type=jnp.float32,
        ).reshape(tile_group, TILE, width)
        run_max, run_sum, run_acc = carried
        for member in range(tile_group):
            offset = row_ids[member] * TILE
            old_max = lax.dynamic_slice_in_dim(run_max, offset, TILE, 1)
            old_sum = lax.dynamic_slice_in_dim(run_sum, offset, TILE, 1)
            old_acc = lax.dynamic_slice_in_dim(run_acc, offset, TILE, 0)
            new_max = jnp.maximum(old_max, tile_max[member])
            keep_factor = jnp.exp(old_max - new_max)
            fresh_factor = jnp.exp(tile_max[member] - new_max)
            run_max = lax.dynamic_update_slice_in_dim(run_max, new_max, offset, 1)
            run_sum = lax.dynamic_update_slice_in_dim(
                run_sum, old_sum * keep_factor + tile_sum[member] * fresh_factor, offset, 1
            )
            new_acc = old_acc * head_scale(keep_factor, head_size) + tile_acc[member] * head_scale(
                fresh_factor, head_size
            )
            run_acc = lax.dynamic_update_slice_in_dim(run_acc, new_acc, offset, 0)
        return (run_max, run_sum, run_acc)

    steps_needed = (tile_count + tile_group - 1) // tile_group
    return lax.fori_loop(0, steps_needed, step_group, start_state)


def per_device(points, w_query, w_key, w_value, w_out, gain, cell_counts, tile_slots, edge_masks):
    node_rows = points.shape[0]
    width = points.shape[1]
    head_size = width // HEADS
    score_scale = 1.0 / math.sqrt(head_size)
    tangent = log_map(points)
    own_query = project(tangent, w_query)
    queries = lax.all_gather(own_query, "src", axis=0, tiled=True)
    own_key = project(tangent, w_key)
    own_value = project(tangent, w_value)
    key_rows, value_rows = (
        lax.all_gather(own_key, "dst", axis=0, tiled=True),
        lax.all_gather(own_value, "dst", axis=0, tiled=True),
    )
    run_max, run_sum, run_acc = attend_cell(
        queries, key_rows, value_rows, cell_counts[0, 0], tile_slots[0, 0], edge_masks[0, 0]
    )
    parts_count = lax.axis_size("src")
    max_parts = run_max.reshape(HEADS, parts_count, node_rows).transpose(1, 0, 2)
    sum_parts = run_sum.reshape(HEADS, parts_count, node_rows).transpose(1, 0, 2)
    acc_parts = run_acc.reshape(parts_count, node_rows, width)
    max_parts, sum_parts, acc_parts = (
        lax.all_to_all(max_parts, "src", split_axis=0, concat_axis=0, tiled=True),
        lax.all_to_all(sum_parts, "src", split_axis=0, concat_axis=0, tiled=True),
        lax.all_to_all(acc_parts, "src", split_axis=0, concat_axis=0, tiled=True),
    )
    part_max = jnp.max(max_parts, axis=0)
    factors = jnp.exp(max_parts - part_max[None])
    part_sum = jnp.sum(sum_parts * factors, axis=0)
    part_acc = jnp.sum(
        acc_parts * jnp.repeat(factors.transpose(0, 2, 1), head_size, axis=2), axis=0
    )
    self_prod = own_query.astype(jnp.float32) * own_key.astype(jnp.float32)
    self_score = jnp.sum(self_prod.reshape(node_rows, HEADS, head_size), axis=-1).T * score_scale
    new_max = jnp.maximum(part_max, self_score)
    keep_factor = jnp.exp(part_max - new_max)
    self_exp = jnp.exp(self_score - new_max)
    total_sum = part_sum * keep_factor + self_exp
    self_weight = lax.optimization_barrier(self_exp.astype(jnp.bfloat16)).astype(jnp.float32)
    numerator = part_acc * head_scale(keep_factor, head_size) + head_scale(
        self_weight, head_size
    ) * own_value.astype(jnp.float32)
    mixed = (numerator / head_scale(total_sum, head_size)).astype(jnp.bfloat16)
    shifted = tangent.astype(jnp.float32) + jnp.dot(
        mixed, w_out, preferred_element_type=jnp.float32
    )
    normed = shifted / jnp.sqrt(jnp.mean(shifted * shifted, axis=-1, keepdims=True) + 1e-06) * gain
    return exp_map(normed)


def solution(mesh):
    return jax.shard_map(
        per_device,
        mesh=mesh,
        in_specs=(
            P(("dst", "src"), None),
            P(),
            P(),
            P(),
            P(),
            P(),
            P("dst", "src"),
            P("dst", "src", None),
            P("dst", "src", None, None, None),
        ),
        out_specs=P(("dst", "src"), None),
        check_vma=False,
    )
```

profile of v0, /device:TPU:0, one launch (start us, length us, event | category | flops | bytes accessed | tf_op | source)
XLA Modules:
  0.0 154.6 jit_solution(15205667748200057857)
XLA Ops:
  1.7 1.1 convolution_convert_fusion.2
  2.8 15.6 %all_gather.9 = bf16[512,256]{1,0:T(8,128)(2,1)S(1)} all-gather(bf16[128,256]{1,0:T(8,128)(2,1)S(1)} %convolution_convert_fusion.2), channel_id=1, replica_groups=mesh['dst'=8,'src'=4] {'src'}, dimensions={0}, use_global_device_ids=true | all-gather | bytes 327680 | tf_op jit(solution)/shard_map/all_gather | solution.py:108
  19.3 9.8 %all_gather.10 = bf16[1024,256]{1,0:T(8,128)(2,1)S(1)} all-gather(bf16[128,256]{1,0:T(8,128)(2,1)S(1)} %get-tuple-element.250), channel_id=1, replica_groups=mesh['dst'=8,'src'=4] {'dst'}, dimensions={0}, use_global_device_ids=true | all-gather | bytes 589824 | tf_op jit(solution)/shard_map/all_gather | solution.py:112
  30.3 9.8 %all_gather.11 = bf16[1024,256]{1,0:T(8,128)(2,1)S(1)} all-gather(bf16[128,256]{1,0:T(8,128)(2,1)S(1)} %convolution_convert_fusion), channel_id=1, replica_groups=mesh['dst'=8,'src'=4] {'dst'}, dimensions={0}, use_global_device_ids=true | all-gather | bytes 589824 | tf_op jit(solution)/shard_map/all_gather | solution.py:113
  40.2 1.4 reshape.215
  41.9 1.3 copy.52
  44.5 36.5 %while.16 = (s32[]{:T(128)}, f32[4,512]{1,0:T(4,128)}, f32[4,512]{1,0:T(4,128)}, f32[512,256]{0,1:T(8,128)S(1)}, s32[]{:T(128)}, /*index=5*/s32[16]{0:T(128)S(1)...) while((s32[]{:T(128)}, f32[4,512]{1,0:T(4,128)}, ...), condition=%wide.region_4.5_spmd, body=%wide.region_1.4_spmd.sunk | while | flops 70004856 | bytes 13525715 | solution.py:98
  45.2 1.1 fusion.84
  48.9 2.2 %gather_fusion.2 = bf16[4,128,4,64]{3,2,1,0:T(4,128)(2,1)S(1)} fusion(bf16[8,128,4,64]{3,2,1,0:T(4,128)(2,1)} %get-tuple-element.431, s32[1024]{0:T(1024)S(1)} %pad_clamp_fusion.4), kind=kCustom, calls=%fused_computation.2.clone.1 | custom fusion | bytes 524304 | tf_op jit(solution)/shard_map/while/body/gather | solution.py:62
  53.7 1.3 fusion.88
  56.2 1.2 fusion.90
  58.8 1.3 fusion.92
  61.4 1.2 fusion.94
  67.1 2.2 %gather_fusion.2 = bf16[4,128,4,64]{3,2,1,0:T(4,128)(2,1)S(1)} fusion(bf16[8,128,4,64]{3,2,1,0:T(4,128)(2,1)} %get-tuple-element.431, s32[1024]{0:T(1024)S(1)} %pad_clamp_fusion.4), kind=kCustom, calls=%fused_computation.2.clone.1 | custom fusion | bytes 524304 | tf_op jit(solution)/shard_map/while/body/gather | solution.py:62
  71.9 1.3 fusion.88
  74.4 1.3 fusion.90
  77.0 1.3 fusion.92
  79.6 1.3 fusion.94
  81.0 41.9 %all-to-all-start.1 = ((f32[4,4,128]{2,1,0:T(4,128)}), f32[4,4,128]{2,1,0:T(4,128)S(1)}, u32[]{:S(2)}, u32[]{:S(2)}) async-start(f32[4,4,128]{2,1,0:T(4,128)} %bitcast.38), calls=%async_computation.1 | async-start | bytes 16384 | tf_op jit(solution)/shard_map/all_to_all | solution.py:123
  123.0 5.5 %all-to-all-done.1 = f32[4,4,128]{2,1,0:T(4,128)S(1)} async-done(((f32[4,4,128]{2,1,0:T(4,128)}), f32[4,4,128]{2,1,0:T(4,128)S(1)}, u32[]{:S(2)}, u32[]{:S(2)}) %all-to-all-start.1) | async-done | bytes 8224 | tf_op jit(solution)/shard_map/all_to_all | solution.py:123
  128.5 3.3 %all-to-all-start.2 = ((f32[4,4,128]{2,1,0:T(4,128)}), f32[4,4,128]{2,1,0:T(4,128)S(1)}, u32[]{:S(2)}, u32[]{:S(2)}) async-start(f32[4,4,128]{2,1,0:T(4,128)} %bitcast.48), calls=%async_computation.2 | async-start | bytes 16384 | tf_op jit(solution)/shard_map/all_to_all | solution.py:124
  133.0 4.3 %all-to-all-done.2 = f32[4,4,128]{2,1,0:T(4,128)S(1)} async-done(((f32[4,4,128]{2,1,0:T(4,128)}), f32[4,4,128]{2,1,0:T(4,128)S(1)}, u32[]{:S(2)}, u32[]{:S(2)}) %all-to-all-start.2) | async-done | bytes 8224 | tf_op jit(solution)/shard_map/all_to_all | solution.py:124
  137.3 3.5 %all-to-all-start = ((f32[4,128,256]{1,2,0:T(8,128)}), f32[4,128,256]{1,2,0:T(8,128)S(1)}, u32[]{:S(2)}, u32[]{:S(2)}) async-start(f32[4,128,256]{1,2,0:T(8,128)} %copy.60), calls=%async_computation | async-start | bytes 1048576 | tf_op jit(solution)/shard_map/all_to_all | solution.py:125
  141.2 10.4 %all-to-all-done = f32[4,128,256]{1,2,0:T(8,128)S(1)} async-done(((f32[4,128,256]{1,2,0:T(8,128)}), f32[4,128,256]{1,2,0:T(8,128)S(1)}, u32[]{:S(2)}, u32[]{:S(2)}) %all-to-all-start) | async-done | bytes 524320 | tf_op jit(solution)/shard_map/all_to_all | solution.py:125
  (102 shorter events, 24.8 us)
Async XLA Ops:
  0.0 18.5 %copy-start = (bf16[256,256]{1,0:T(8,128)(2,1)S(1)}, bf16[256,256]{1,0:T(8,128)(2,1)}, u32[]{:S(2)}) copy-start(bf16[256,256]{1,0:T(8,128)(2,1)} %param.13) | copy-start | bytes 393220
  0.0 1.7 %copy-start.7 = (bf16[128,256]{1,0:T(8,128)(2,1)S(1)}, bf16[128,256]{1,0:T(8,128)(2,1)}, u32[]{:S(2)}) copy-start(bf16[128,256]{1,0:T(8,128)(2,1)} %param.11) | copy-start | bytes 196612
  29.2 0.9 copy-start.11
  30.3 9.9 %copy-start.5 = (bf16[128,256]{1,0:T(8,128)(2,1)}, bf16[128,256]{1,0:T(8,128)(2,1)S(1)}, u32[]{:S(2)}) copy-start(bf16[128,256]{1,0:T(8,128)(2,1)S(1)} %convolution_convert_fusion) | copy-start | bytes 196612
  40.2 1.7 %copy-start.3 = (s32[1,1,16,128,128]{4,3,2,1,0:T(8,128)S(1)}, s32[1,1,16,128,128]{4,3,2,1,0:T(8,128)}, u32[]{:S(2)}) copy-start(s32[1,1,16,128,128]{4,3,2,1,0:T(8,128)} %param.19) | copy-start | bytes 3145732
  43.8 0.7 copy-start.9
  44.5 78.4 %copy-start.4 = (f32[128,256]{1,0:T(8,128)S(1)}, f32[128,256]{1,0:T(8,128)}, u32[]{:S(2)}) copy-start(f32[128,256]{1,0:T(8,128)} %get-tuple-element.249) | copy-start | bytes 393220
  44.5 2.9 %copy-start.1 = (bf16[8,128,4,64]{3,2,1,0:T(4,128)(2,1)}, bf16[8,128,4,64]{3,2,1,0:T(4,128)(2,1)S(1)}, u32[]{:S(2)}) copy-start(bf16[8,128,4,64]{3,2,1,0:T(4,128)(2,1)S(1)} %get-tuple-element.430) | copy-start | bytes 1572868 | tf_op jit(solution)/shard_map/while
  51.7 11.0 %copy-start.2 = (bf16[8,128,4,64]{3,2,1,0:T(4,128)(2,1)S(1)}, bf16[8,128,4,64]{3,2,1,0:T(4,128)(2,1)}, u32[]{:S(2)}) copy-start(bf16[8,128,4,64]{3,2,1,0:T(4,128)(2,1)} %copy-done.1) | copy-start | bytes 1572868 | tf_op jit(solution)/shard_map/while
  62.7 2.9 %copy-start.1 = (bf16[8,128,4,64]{3,2,1,0:T(4,128)(2,1)}, bf16[8,128,4,64]{3,2,1,0:T(4,128)(2,1)S(1)}, u32[]{:S(2)}) copy-start(bf16[8,128,4,64]{3,2,1,0:T(4,128)(2,1)S(1)} %get-tuple-element.430) | copy-start | bytes 1572868 | tf_op jit(solution)/shard_map/while
  70.0 11.0 %copy-start.2 = (bf16[8,128,4,64]{3,2,1,0:T(4,128)(2,1)S(1)}, bf16[8,128,4,64]{3,2,1,0:T(4,128)(2,1)}, u32[]{:S(2)}) copy-start(bf16[8,128,4,64]{3,2,1,0:T(4,128)(2,1)} %copy-done.1) | copy-start | bytes 1572868 | tf_op jit(solution)/shard_map/while
  81.0 47.5 %all-to-all-start.1 = ((f32[4,4,128]{2,1,0:T(4,128)}), f32[4,4,128]{2,1,0:T(4,128)S(1)}, u32[]{:S(2)}, u32[]{:S(2)}) async-start(f32[4,4,128]{2,1,0:T(4,128)} %bitcast.38), calls=%async_computation.1 | async-start | bytes 16384 | tf_op jit(solution)/shard_map/all_to_all | solution.py:123
  128.5 8.8 %all-to-all-start.2 = ((f32[4,4,128]{2,1,0:T(4,128)}), f32[4,4,128]{2,1,0:T(4,128)S(1)}, u32[]{:S(2)}, u32[]{:S(2)}) async-start(f32[4,4,128]{2,1,0:T(4,128)} %bitcast.48), calls=%async_computation.2 | async-start | bytes 16384 | tf_op jit(solution)/shard_map/all_to_all | solution.py:124
  137.3 14.3 %all-to-all-start = ((f32[4,128,256]{1,2,0:T(8,128)}), f32[4,128,256]{1,2,0:T(8,128)S(1)}, u32[]{:S(2)}, u32[]{:S(2)}) async-start(f32[4,128,256]{1,2,0:T(8,128)} %copy.60), calls=%async_computation | async-start | bytes 1048576 | tf_op jit(solution)/shard_map/all_to_all | solution.py:125
  151.6 0.8 copy-start.6
  151.7 0.9 copy-start.8
  151.7 1.0 copy-start.12
  152.9 0.7 copy-start.10
where the time goes:
time: 156 us; the launch traced here: 155 us
  starting transfers between devices  48.6 us (31%)
  blocking collectives  35.3 us (23%)
  other arithmetic  22.1 us (14%)
  waiting for transfers between devices  20.2 us (13%)
  local copies, waits for them, and re-layouts  18.1 us (12%)
  loops' own time  5.1 us (3%)
  matrix products  4.16 us (3%)
    all_to_all x1, starting transfers between devices, per_device(): lax.all_to_all(max_parts, 'src', split_axis=0, concat_axis=0, tiled=True)  41.9 us
    all_gather x1, blocking collectives, per_device(): queries = lax.all_gather(own_query, 'src', axis=0, tiled=True)  15.6 us
    transpose x17, other arithmetic, head_scale(): return jnp.repeat(factor.T, head_size, axis=1)  15.5 us
    all_to_all x1, waiting for transfers between devices, per_device(): lax.all_to_all(acc_parts, 'src', split_axis=0, concat_axis=0, tiled=True)  10.4 us
    all_gather x1, blocking collectives, per_device(): lax.all_gather(own_key, 'dst', axis=0, tiled=True)  9.85 us
    all_gather x1, blocking collectives, per_device(): lax.all_gather(own_value, 'dst', axis=0, tiled=True)  9.85 us
    all_to_all x1, waiting for transfers between devices, per_device(): lax.all_to_all(max_parts, 'src', split_axis=0, concat_axis=0, tiled=True)  5.49 us
    another operation x1, loops' own time, attend_cell(): return lax.fori_loop(0, steps_needed, step_group, start_state)  5.1 us
  transfers between devices with their start and end apart: 3, of which 3 were waited for; matrix products, arithmetic and copies ran while one was open for 1% of the time, Pallas kernels for 0%

commit v1 on v0

v1 whole, which is shorter than its diff:
```python
import functools
import math

import jax
import jax.numpy as jnp
from jax import lax
from jax.experimental import pallas as pl
from jax.experimental.pallas import tpu as pltpu
from jax.sharding import PartitionSpec as P

HEADS = 4
NEG = -1e30
MESH = pl.DeviceIdType.MESH


def dot(a, b, dims=((1,), (0,))):
    return lax.dot_general(a, b, (dims, ((), ())), preferred_element_type=jnp.float32)


def log_map(points):
    values_f = points.astype(jnp.float32)
    radius = jnp.sqrt(jnp.sum(values_f * values_f, axis=-1, keepdims=True) + 1e-06)
    root_width = math.sqrt(points.shape[-1])
    ratio = radius / root_width
    arc = jnp.log(ratio + jnp.sqrt(ratio * ratio + 1.0))
    return (values_f * (root_width * arc / radius)).astype(jnp.bfloat16)


def sinh_over(x):
    sq = x * x
    series = 1.0 + sq / 6.0 * (1.0 + sq / 20.0 * (1.0 + sq / 42.0 * (1.0 + sq / 72.0)))
    grown = jnp.exp(x)
    return jnp.where(x < 1.0, series, 0.5 * (grown - 1.0 / grown) / x)


def fold_rows(x):
    return x.reshape(x.shape[0] // 8, 8, x.shape[1])


def kernel(
    n_dst, n_src, tile, n_slots,
    points_ref, wq_ref, wk_ref, wv_ref, wo_ref, gain_ref, counts_ref, slots_ref, masks_hbm,
    out_ref,
    kt, qt, masks, bias, inv, k_all, v_all, scores, probs, acc_out, stat_out, acc_in, stat_in,
    mask_sem, kt_send, kt_recv, qt_send, qt_recv, acc_send, acc_recv, stat_send, stat_recv,
):
    d = lax.axis_index("dst")
    s = lax.axis_index("src")
    width = points_ref.shape[1]
    head = width // HEADS
    scale = 1.0 / math.sqrt(head)

    def dst_peer(off):
        return lax.rem(d + off, n_dst)

    def src_peer(off):
        return lax.rem(s + off, n_src)

    barrier = pltpu.get_barrier_semaphore()
    for off in range(1, n_src):
        pl.semaphore_signal(barrier, inc=1, device_id=(d, src_peer(off)), device_id_type=MESH)
    for off in range(1, n_dst):
        pl.semaphore_signal(barrier, inc=1, device_id=(dst_peer(off), s), device_id_type=MESH)

    mask_copy = pltpu.make_async_copy(masks_hbm, masks, mask_sem)
    mask_copy.start()
    tangent = log_map(points_ref[...])
    kt[d] = tangent
    qt[s] = tangent
    pl.semaphore_wait(barrier, n_src - 1 + n_dst - 1)

    def q_copy(slot, peer):
        return pltpu.make_async_remote_copy(
            src_ref=qt.at[slot], dst_ref=qt.at[slot],
            send_sem=qt_send.at[peer], recv_sem=qt_recv.at[slot],
            device_id=(d, peer), device_id_type=MESH)

    def k_copy(slot, peer):
        return pltpu.make_async_remote_copy(
            src_ref=kt.at[slot], dst_ref=kt.at[slot],
            send_sem=kt_send.at[peer], recv_sem=kt_recv.at[slot],
            device_id=(peer, s), device_id_type=MESH)

    src_order = [2, 1, 3] if n_src == 4 else list(range(1, n_src))
    for off in src_order:
        q_copy(s, src_peer(off)).start()
    for off in range(1, n_dst):
        k_copy(d, dst_peer(off)).start()

    own_q = dot(tangent, wq_ref[...]).astype(jnp.bfloat16).astype(jnp.float32).T
    own_k = dot(tangent, wk_ref[...]).astype(jnp.bfloat16).astype(jnp.float32).T
    own_v = dot(tangent, wv_ref[...]).T.astype(jnp.bfloat16).astype(jnp.float32)
    self_score = [
        jnp.sum((own_q * own_k)[h * head:(h + 1) * head], axis=0, keepdims=True) * scale
        for h in range(HEADS)
    ]

    count = counts_ref[0]

    def find_slot(index, carry):
        found = jnp.int32(n_slots)
        for t in range(n_slots):
            found = jnp.where((slots_ref[t] == index) & (count > t), jnp.int32(t), found)
        inv[index] = found
        return carry

    lax.fori_loop(0, n_src * n_dst, find_slot, 0)

    mask_copy.wait()
    bias[n_slots] = jnp.full((tile, tile), NEG, jnp.float32)

    def turn_mask(t, carry):
        bias[t] = jnp.where(masks[t] == 1, 0.0, NEG).astype(jnp.float32).T
        return carry

    lax.fori_loop(0, n_slots, turn_mask, 0)

    def project_slot(slot):
        rows = kt[slot]
        at = pl.ds(pl.multiple_of(slot * tile, tile), tile)
        k_all[at, :] = dot(rows, wk_ref[...]).astype(jnp.bfloat16)
        v_all[:, at] = dot(rows, wv_ref[...]).T.astype(jnp.bfloat16)

    project_slot(d)

    def take_keys(off, carry):
        slot = dst_peer(off)
        k_copy(slot, slot).wait_recv()
        project_slot(slot)
        return carry

    lax.fori_loop(1, n_dst, take_keys, 0)

    group = min(8, n_dst)
    feature_head = lax.broadcasted_iota(jnp.int32, (tile, width), 1) // head

    def over_groups(body, start):
        if n_dst == group:
            return body(0, start)
        return lax.fori_loop(0, n_dst // group, body, start)

    def attend(r):
        q = dot(qt[r], wq_ref[...]).astype(jnp.bfloat16).astype(jnp.float32) * scale
        q_heads = jnp.concatenate(
            [jnp.where(feature_head == h, q, 0.0).astype(jnp.bfloat16) for h in range(HEADS)], axis=0)

        def score_group(g, tops):
            tops = list(tops)
            for member in range(group):
                k = g * group + member
                at = pl.ds(k * tile, tile) if isinstance(k, int) else pl.ds(pl.multiple_of(k * tile, tile), tile)
                prod = dot(k_all[at, :], q_heads, ((1,), (1,)))
                term = bias[inv[r * n_dst + k]]
                for h in range(HEADS):
                    part = prod[:, h * tile:(h + 1) * tile] + term
                    scores[at, h * tile:(h + 1) * tile] = part
                    tops[h] = jnp.maximum(tops[h], jnp.max(fold_rows(part), axis=0))
            return tuple(tops)

        tops = over_groups(score_group, tuple(jnp.full((8, tile), NEG, jnp.float32) for _ in range(HEADS)))
        tops = [jnp.max(t, axis=0, keepdims=True) for t in tops]

        def exp_group(g, sums):
            sums = list(sums)
            for member in range(group):
                k = g * group + member
                at = pl.ds(k * tile, tile) if isinstance(k, int) else pl.ds(pl.multiple_of(k * tile, tile), tile)
                for h in range(HEADS):
                    lanes = slice(h * tile, (h + 1) * tile)
                    p = jnp.exp(scores[at, lanes] - tops[h])
                    sums[h] = sums[h] + jnp.sum(fold_rows(p), axis=0)
                    probs[at, lanes] = p.astype(jnp.bfloat16)
            return tuple(sums)

        sums = over_groups(exp_group, tuple(jnp.zeros((8, tile), jnp.float32) for _ in range(HEADS)))
        sums = [jnp.sum(t, axis=0, keepdims=True) for t in sums]
        accs = []
        for j in range(HEADS // 2):
            both = dot(v_all[2 * j * head:2 * (j + 1) * head, :], probs[:, 2 * j * tile:2 * (j + 1) * tile])
            accs.append(both[:head, :tile])
            accs.append(both[head:, tile:])
        return tops, sums, accs

    def acc_copy(slot, peer):
        return pltpu.make_async_remote_copy(
            src_ref=acc_out.at[peer], dst_ref=acc_in.at[slot],
            send_sem=acc_send.at[peer], recv_sem=acc_recv.at[slot],
            device_id=(d, peer), device_id_type=MESH)

    def stat_copy(slot, peer):
        return pltpu.make_async_remote_copy(
            src_ref=stat_out.at[peer], dst_ref=stat_in.at[slot],
            send_sem=stat_send.at[peer], recv_sem=stat_recv.at[slot],
            device_id=(d, peer), device_id_type=MESH)

    for off in src_order:
        r = src_peer(off)
        q_copy(r, r).wait_recv()
        tops, sums, accs = attend(r)
        stat_out[r] = jnp.concatenate(tops + sums, axis=0)
        acc_out[r] = jnp.concatenate(accs, axis=0).astype(jnp.bfloat16)
        acc_copy(s, r).start()
        stat_copy(s, r).start()

    tops, sums, accs = attend(s)
    parts = [(tops, sums, accs)]
    for off in src_order:
        c = src_peer(off)
        acc_copy(c, c).wait_recv()
        stat_copy(c, c).wait_recv()
        stat = stat_in[c]
        acc = acc_in[c].astype(jnp.float32)
        parts.append((
            [stat[h:h + 1] for h in range(HEADS)],
            [stat[HEADS + h:HEADS + h + 1] for h in range(HEADS)],
            [acc[h * head:(h + 1) * head] for h in range(HEADS)],
        ))

    mixed = []
    for h in range(HEADS):
        top = self_score[h]
        for tops, _, _ in parts:
            top = jnp.maximum(top, tops[h])
        weight = jnp.exp(self_score[h] - top)
        total = weight
        number = weight.astype(jnp.bfloat16).astype(jnp.float32) * own_v[h * head:(h + 1) * head]
        for tops, sums, accs in parts:
            factor = jnp.exp(tops[h] - top)
            total = total + sums[h] * factor
            number = number + accs[h] * factor
        mixed.append(number / total)
    mixed = jnp.concatenate(mixed, axis=0).T.astype(jnp.bfloat16)
    shifted = tangent.astype(jnp.float32) + dot(mixed, wo_ref[...])
    square = jnp.mean(shifted * shifted, axis=-1, keepdims=True)
    normed = shifted * (1.0 / jnp.sqrt(square + 1e-06)) * gain_ref[...]
    radius = jnp.sqrt(jnp.sum(normed * normed, axis=-1, keepdims=True) + 1e-06)
    out_ref[...] = (normed * sinh_over(radius * (1.0 / math.sqrt(width)))).astype(jnp.bfloat16)

    for off in range(1, n_dst):
        k_copy(d, dst_peer(off)).wait_send()
    for off in src_order:
        r = src_peer(off)
        q_copy(s, r).wait_send()
        acc_copy(s, r).wait_send()
        stat_copy(s, r).wait_send()


def per_device(n_dst, n_src, points, w_query, w_key, w_value, w_out, gain, cell_counts, tile_slots, edge_masks):
    tile = points.shape[0]
    width = points.shape[1]
    n_slots = tile_slots.shape[-1]
    vmem = pl.BlockSpec(memory_space=pltpu.VMEM)
    smem = pl.BlockSpec(memory_space=pltpu.SMEM)
    dma = pltpu.SemaphoreType.DMA
    return pl.pallas_call(
        functools.partial(kernel, n_dst, n_src, tile, n_slots),
        out_shape=jax.ShapeDtypeStruct((tile, width), jnp.bfloat16),
        in_specs=[vmem] * 6 + [smem, smem, pl.BlockSpec(memory_space=pl.ANY)],
        out_specs=vmem,
        scratch_shapes=[
            pltpu.VMEM((n_dst, tile, width), jnp.bfloat16),
            pltpu.VMEM((n_src, tile, width), jnp.bfloat16),
            pltpu.VMEM((n_slots, tile, tile), jnp.int32),
            pltpu.VMEM((n_slots + 1, tile, tile), jnp.float32),
            pltpu.SMEM((n_src * n_dst,), jnp.int32),
            pltpu.VMEM((n_dst * tile, width), jnp.bfloat16),
            pltpu.VMEM((width, n_dst * tile), jnp.bfloat16),
            pltpu.VMEM((n_dst * tile, HEADS * tile), jnp.float32),
            pltpu.VMEM((n_dst * tile, HEADS * tile), jnp.bfloat16),
            pltpu.VMEM((n_src, width, tile), jnp.bfloat16),
            pltpu.VMEM((n_src, 2 * HEADS, tile), jnp.float32),
            pltpu.VMEM((n_src, width, tile), jnp.bfloat16),
            pltpu.VMEM((n_src, 2 * HEADS, tile), jnp.float32),
            dma,
            dma((n_dst,)), dma((n_dst,)),
            dma((n_src,)), dma((n_src,)),
            dma((n_src,)), dma((n_src,)),
            dma((n_src,)), dma((n_src,)),
        ],
        compiler_params=pltpu.CompilerParams(
            collective_id=0, has_side_effects=True, vmem_limit_bytes=44 * 1024 * 1024),
    )(
        points, w_query, w_key, w_value, w_out, gain.reshape(1, width),
        cell_counts.reshape(1), tile_slots.reshape(n_slots), edge_masks.reshape(n_slots, tile, tile),
    )


def solution(mesh):
    return jax.shard_map(
        functools.partial(per_device, mesh.shape["dst"], mesh.shape["src"]),
        mesh=mesh,
        in_specs=(
            P(("dst", "src"), None),
            P(),
            P(),
            P(),
            P(),
            P(),
            P("dst", "src"),
            P("dst", "src", None),
            P("dst", "src", None, None, None),
        ),
        out_specs=P(("dst", "src"), None),
        check_vma=False,
    )
```

time: 156 us -> 33 us (0.21)
  starting transfers between devices: 48.6 us -> 0 us
  blocking collectives: 35.3 us -> 0 us
  Pallas kernels: 0 us -> 25.1 us
  other arithmetic: 22.1 us -> 0 us
  waiting for transfers between devices: 20.2 us -> 0 us
  local copies, waits for them, and re-layouts: 18.1 us -> 6.98 us
  loops' own time: 5.1 us -> 0 us
  matrix products: 4.16 us -> 0 us
    all_to_all x3 -> x0, starting transfers between devices: 48.6 us -> none  [the longest x1 41.9 us: per_device(): lax.all_to_all(max_parts, 'src', split_axis=0, concat_axis=0, tiled=True)]
    all_gather x3 -> x0, blocking collectives: 35.3 us -> none  [the longest x1 15.6 us: per_device(): queries = lax.all_gather(own_query, 'src', axis=0, tiled=True)]
    pallas_call x0 -> x1, Pallas kernels: none -> 25.1 us  [per_device(): pl.pallas_call(functools.partial(kernel, n_dst, n_src, tile, n_slots), ou...]
    all_to_all x3 -> x0, waiting for transfers between devices: 20.2 us -> none  [the longest x1 10.4 us: per_device(): lax.all_to_all(acc_parts, 'src', split_axis=0, concat_axis=0, tiled=True)]
    transpose x18 -> x0, other arithmetic: 15.6 us -> none  [the longest x17 15.5 us: head_scale(): return jnp.repeat(factor.T, head_size, axis=1)]
    gather x6 -> x0, local copies, waits for them, and re-layouts: 8.41 us -> none  [the longest x2 4.44 us: step_group(): v_group = v_tiles[col_ids]]
    another operation x1 -> x0, loops' own time: 5.1 us -> none  [attend_cell(): return lax.fori_loop(0, steps_needed, step_group, start_state)]
    dot_general x8 -> x0, matrix products: 4.16 us -> none  [the longest x3 2.21 us: project(): jnp.dot(rows, weight, preferred_element_type=jnp.float32)]
  transfers between devices with their start and end apart: 3 -> 0, of which waited for: 3 -> 0; matrix products, arithmetic and copies ran while one was open for 1% -> 0% of each run, Pallas kernels for 0% -> 0%
where the time goes in v1:
time: 33 us; the launch traced here: 32.7 us
  Pallas kernels  25.1 us (76%)
  local copies, waits for them, and re-layouts  6.98 us (21%)
  between operations  0.68 us (2%)
    pallas_call x1, Pallas kernels, per_device(): pl.pallas_call(functools.partial(kernel, n_dst, n_src, tile, n_slots), ou...  25.1 us
    unnamed x17, local copies, waits for them, and re-layouts  6.98 us

profile of v1, /device:TPU:0, one launch (start us, length us, event | category | flops | bytes accessed | tf_op | source)
XLA Modules:
  0.0 32.7 jit_solution(4733183875549772899)
XLA Ops:
  0.7 0.0 copy-start.6
  0.7 0.0 copy-start.7
  0.7 0.7 %copy-done.6 = f32[256]{0:T(256)S(1)} copy-done((f32[256]{0:T(256)S(1)}, f32[256]{0:T(256)}, u32[]{:S(2)}) %copy-start.6) | copy-done | bytes 1048
  1.3 0.0 copy-done.7
  1.3 0.0 copy-start
  1.3 1.2 %copy-done = s32[1,1,16,128,128]{4,3,2,1,0:T(8,128)S(1)} copy-done((s32[1,1,16,128,128]{4,3,2,1,0:T(8,128)S(1)}, s32[1,1,16,128,128]{4,3,2,1,0:T(8,128)}, u32[]{:S(2)}) %copy-start) | copy-done | bytes 1048600
  2.6 0.0 copy-start.1
  2.6 0.9 %copy-done.1 = bf16[256,256]{1,0:T(8,128)(2,1)S(1)} copy-done((bf16[256,256]{1,0:T(8,128)(2,1)S(1)}, bf16[256,256]{1,0:T(8,128)(2,1)}, u32[]{:S(2)}) %copy-start.1) | copy-done | bytes 131096
  3.5 0.0 copy-start.2
  3.5 0.9 %copy-done.2 = bf16[256,256]{1,0:T(8,128)(2,1)S(1)} copy-done((bf16[256,256]{1,0:T(8,128)(2,1)S(1)}, bf16[256,256]{1,0:T(8,128)(2,1)}, u32[]{:S(2)}) %copy-start.2) | copy-done | bytes 131096
  4.4 0.0 copy-start.3
  4.4 0.9 %copy-done.3 = bf16[256,256]{1,0:T(8,128)(2,1)S(1)} copy-done((bf16[256,256]{1,0:T(8,128)(2,1)S(1)}, bf16[256,256]{1,0:T(8,128)(2,1)}, u32[]{:S(2)}) %copy-start.3) | copy-done | bytes 131096
  5.3 0.0 copy-start.4
  5.3 0.9 %copy-done.4 = bf16[256,256]{1,0:T(8,128)(2,1)S(1)} copy-done((bf16[256,256]{1,0:T(8,128)(2,1)S(1)}, bf16[256,256]{1,0:T(8,128)(2,1)}, u32[]{:S(2)}) %copy-start.4) | copy-done | bytes 131096
  6.2 0.0 copy-start.5
  6.2 0.8 %copy-done.5 = bf16[128,256]{1,0:T(8,128)(2,1)S(1)} copy-done((bf16[128,256]{1,0:T(8,128)(2,1)S(1)}, bf16[128,256]{1,0:T(8,128)(2,1)}, u32[]{:S(2)}) %copy-start.5) | copy-done | bytes 65560
  7.0 25.1 %shard_map.91 = bf16[128,256]{1,0:T(8,128)(2,1)S(1)} custom-call(bf16[128,256]{1,0:T(8,128)(2,1)S(1)} %copy-done.5, bf16[256,256]{1,0:T(8,128)(2,1)S(1)} %copy-done.1, bf16[256,256]{1,0:T(8,128)(2,1)S(1)} %copy-done.2, bf16[256,256]{1,0:T(8,128)(2,1)S(1)} %copy-done.3, bf16[256,256]{1,0:T(8,128)(2,1)S(1)} %copy-done.4, f32[1,256]{1,0:T(1,128)S(1)} %bitcast.6, ...), custom_call_target="tpu_custom_call" | custom-call | tf_op jit(solution)/shard_map/pallas_call | solution.py:255
  32.1 0.6 %copy.12 = bf16[128,256]{1,0:T(8,128)(2,1)} copy(bf16[128,256]{1,0:T(8,128)(2,1)S(1)} %shard_map.91) | data formatting | bytes 131072
Async XLA Ops:
  0.7 0.7 %copy-start.6 = (f32[256]{0:T(256)S(1)}, f32[256]{0:T(256)}, u32[]{:S(2)}) copy-start(f32[256]{0:T(256)} %param.14) | copy-start | bytes 3076
  0.7 0.7 %copy-start.7 = (s32[1,1,16]{2,1,0:T(1,128)S(1)}, s32[1,1,16]{2,1,0:T(1,128)}, u32[]{:S(2)}) copy-start(s32[1,1,16]{2,1,0:T(1,128)} %param.16) | copy-start | bytes 196
  1.3 1.2 %copy-start = (s32[1,1,16,128,128]{4,3,2,1,0:T(8,128)S(1)}, s32[1,1,16,128,128]{4,3,2,1,0:T(8,128)}, u32[]{:S(2)}) copy-start(s32[1,1,16,128,128]{4,3,2,1,0:T(8,128)} %param.17) | copy-start | bytes 3145732
  2.6 0.9 %copy-start.1 = (bf16[256,256]{1,0:T(8,128)(2,1)S(1)}, bf16[256,256]{1,0:T(8,128)(2,1)}, u32[]{:S(2)}) copy-start(bf16[256,256]{1,0:T(8,128)(2,1)} %wq_ref.1) | copy-start | bytes 393220
  3.5 0.9 %copy-start.2 = (bf16[256,256]{1,0:T(8,128)(2,1)S(1)}, bf16[256,256]{1,0:T(8,128)(2,1)}, u32[]{:S(2)}) copy-start(bf16[256,256]{1,0:T(8,128)(2,1)} %wk_ref.1) | copy-start | bytes 393220
  4.4 0.9 %copy-start.3 = (bf16[256,256]{1,0:T(8,128)(2,1)S(1)}, bf16[256,256]{1,0:T(8,128)(2,1)}, u32[]{:S(2)}) copy-start(bf16[256,256]{1,0:T(8,128)(2,1)} %wv_ref.1) | copy-start | bytes 393220
  5.3 0.9 %copy-start.4 = (bf16[256,256]{1,0:T(8,128)(2,1)S(1)}, bf16[256,256]{1,0:T(8,128)(2,1)}, u32[]{:S(2)}) copy-start(bf16[256,256]{1,0:T(8,128)(2,1)} %wo_ref.1) | copy-start | bytes 393220
  6.2 0.8 %copy-start.5 = (bf16[128,256]{1,0:T(8,128)(2,1)S(1)}, bf16[128,256]{1,0:T(8,128)(2,1)}, u32[]{:S(2)}) copy-start(bf16[128,256]{1,0:T(8,128)(2,1)} %points_ref.1) | copy-start | bytes 196612

commit v2 on v1

--- a/solution.py
+++ b/solution.py
@@ -39,14 +39,15 @@
 
 def kernel(
     n_dst, n_src, tile, n_slots,
-    points_ref, wq_ref, wk_ref, wv_ref, wo_ref, gain_ref, counts_ref, slots_ref, masks_hbm,
+    points_hbm, wq_hbm, wk_hbm, wv_hbm, wo_hbm, gain_hbm, counts_hbm, slots_hbm, masks_hbm,
     out_ref,
-    kt, qt, masks, bias, inv, k_all, v_all, scores, probs, acc_out, stat_out, acc_in, stat_in,
-    mask_sem, kt_send, kt_recv, qt_send, qt_recv, acc_send, acc_recv, stat_send, stat_recv,
+    points_ref, wq_ref, wk_ref, wv_ref, wo_ref, gain_ref, counts_ref, slots_ref, masks,
+    kt, qt, bias, inv, wv_turned, q_heads, k_all, v_all, scores, probs, acc_out, stat_out, acc_in, stat_in,
+    load_sem, kt_send, kt_recv, qt_send, qt_recv, acc_send, acc_recv, stat_send, stat_recv,
 ):
     d = lax.axis_index("dst")
     s = lax.axis_index("src")
-    width = points_ref.shape[1]
+    width = points_hbm.shape[1]
     head = width // HEADS
     scale = 1.0 / math.sqrt(head)
 
@@ -62,8 +63,17 @@
     for off in range(1, n_dst):
         pl.semaphore_signal(barrier, inc=1, device_id=(dst_peer(off), s), device_id_type=MESH)
 
-    mask_copy = pltpu.make_async_copy(masks_hbm, masks, mask_sem)
-    mask_copy.start()
+    loads = [
+        pltpu.make_async_copy(source, target, load_sem.at[index])
+        for index, (source, target) in enumerate([
+            (points_hbm, points_ref), (slots_hbm, slots_ref), (counts_hbm, counts_ref),
+            (wv_hbm, wv_ref), (wk_hbm, wk_ref), (wq_hbm, wq_ref), (masks_hbm, masks),
+            (wo_hbm, wo_ref), (gain_hbm, gain_ref),
+        ])
+    ]
+    for load in loads:
+        load.start()
+    loads[0].wait()
     tangent = log_map(points_ref[...])
     kt[d] = tangent
     qt[s] = tangent
@@ -87,40 +97,54 @@
     for off in range(1, n_dst):
         k_copy(d, dst_peer(off)).start()
 
-    own_q = dot(tangent, wq_ref[...]).astype(jnp.bfloat16).astype(jnp.float32).T
-    own_k = dot(tangent, wk_ref[...]).astype(jnp.bfloat16).astype(jnp.float32).T
-    own_v = dot(tangent, wv_ref[...]).T.astype(jnp.bfloat16).astype(jnp.float32)
-    self_score = [
-        jnp.sum((own_q * own_k)[h * head:(h + 1) * head], axis=0, keepdims=True) * scale
-        for h in range(HEADS)
-    ]
-
-    count = counts_ref[0]
-
-    def find_slot(index, carry):
-        found = jnp.int32(n_slots)
-        for t in range(n_slots):
-            found = jnp.where((slots_ref[t] == index) & (count > t), jnp.int32(t), found)
-        inv[index] = found
+    loads[1].wait()
+    loads[2].wait()
+    count = counts_ref[0, 0]
+    listed = [jnp.where(count > t, slots_ref[0, 0, t], -1) for t in range(n_slots)]
+
+    def find_slots(step, carry):
+        for member in range(4):
+            index = step * 4 + member
+            found = jnp.int32(n_slots)
+            for t in range(n_slots):
+                found = jnp.where(listed[t] == index, jnp.int32(t), found)
+            inv[index] = found
         return carry
 
-    lax.fori_loop(0, n_src * n_dst, find_slot, 0)
-
-    mask_copy.wait()
+    lax.fori_loop(0, n_src * n_dst // 4, find_slots, 0)
+
+    def eye(n):
+        same = lax.broadcasted_iota(jnp.int32, (n, n), 0) == lax.broadcasted_iota(jnp.int32, (n, n), 1)
+        return jnp.where(same, 1.0, 0.0).astype(jnp.bfloat16)
+
+    def turned(x, ident):
+        return dot(ident, x, ((1,), (1,)))
+
+    eye_tile = eye(tile)
+    q_heads[...] = jnp.zeros(q_heads.shape, jnp.bfloat16)
+    loads[3].wait()
+    wv_turned[...] = turned(wv_ref[...], eye(width)).astype(jnp.bfloat16)
+    loads[4].wait()
+    loads[5].wait()
+
+    loads[6].wait()
     bias[n_slots] = jnp.full((tile, tile), NEG, jnp.float32)
 
-    def turn_mask(t, carry):
-        bias[t] = jnp.where(masks[t] == 1, 0.0, NEG).astype(jnp.float32).T
+    def turn_masks(step, carry):
+        for member in range(8):
+            t = step * 8 + member
+            bias[t] = turned(jnp.where(masks[0, 0, t] == 1, 0.0, NEG).astype(jnp.bfloat16), eye_tile)
         return carry
 
-    lax.fori_loop(0, n_slots, turn_mask, 0)
+    lax.fori_loop(0, n_slots // 8, turn_masks, 0)
 
     def project_slot(slot):
         rows = kt[slot]
         at = pl.ds(pl.multiple_of(slot * tile, tile), tile)
         k_all[at, :] = dot(rows, wk_ref[...]).astype(jnp.bfloat16)
-        v_all[:, at] = dot(rows, wv_ref[...]).T.astype(jnp.bfloat16)
-
+        v_all[:, at] = dot(wv_turned[...], rows, ((1,), (1,))).astype(jnp.bfloat16)
+
+    own_v = dot(wv_turned[...], tangent, ((1,), (1,))).astype(jnp.bfloat16).astype(jnp.float32)
     project_slot(d)
 
     def take_keys(off, carry):
@@ -132,7 +156,6 @@
     lax.fori_loop(1, n_dst, take_keys, 0)
 
     group = min(8, n_dst)
-    feature_head = lax.broadcasted_iota(jnp.int32, (tile, width), 1) // head
 
     def over_groups(body, start):
         if n_dst == group:
@@ -140,16 +163,16 @@
         return lax.fori_loop(0, n_dst // group, body, start)
 
     def attend(r):
-        q = dot(qt[r], wq_ref[...]).astype(jnp.bfloat16).astype(jnp.float32) * scale
-        q_heads = jnp.concatenate(
-            [jnp.where(feature_head == h, q, 0.0).astype(jnp.bfloat16) for h in range(HEADS)], axis=0)
+        q = (dot(qt[r], wq_ref[...]).astype(jnp.bfloat16).astype(jnp.float32) * scale).astype(jnp.bfloat16)
+        for h in range(HEADS):
+            q_heads[h * tile:(h + 1) * tile, h * head:(h + 1) * head] = q[:, h * head:(h + 1) * head]
 
         def score_group(g, tops):
             tops = list(tops)
             for member in range(group):
                 k = g * group + member
                 at = pl.ds(k * tile, tile) if isinstance(k, int) else pl.ds(pl.multiple_of(k * tile, tile), tile)
-                prod = dot(k_all[at, :], q_heads, ((1,), (1,)))
+                prod = dot(k_all[at, :], q_heads[...], ((1,), (1,)))
                 term = bias[inv[r * n_dst + k]]
                 for h in range(HEADS):
                     part = prod[:, h * tile:(h + 1) * tile] + term
@@ -203,6 +226,12 @@
         stat_copy(s, r).start()
 
     tops, sums, accs = attend(s)
+    own_prod = dot(k_all[pl.ds(pl.multiple_of(d * tile, tile), tile), :], q_heads[...], ((1,), (1,)))
+    diagonal = lax.broadcasted_iota(jnp.int32, (tile, tile), 0) == lax.broadcasted_iota(jnp.int32, (tile, tile), 1)
+    self_score = [
+        jnp.sum(jnp.where(diagonal, own_prod[:, h * tile:(h + 1) * tile], 0.0), axis=0, keepdims=True)
+        for h in range(HEADS)
+    ]
     parts = [(tops, sums, accs)]
     for off in src_order:
         c = src_peer(off)
@@ -229,7 +258,9 @@
             total = total + sums[h] * factor
             number = number + accs[h] * factor
         mixed.append(number / total)
-    mixed = jnp.concatenate(mixed, axis=0).T.astype(jnp.bfloat16)
+    mixed = turned(jnp.concatenate(mixed, axis=0).astype(jnp.bfloat16), eye_tile).astype(jnp.bfloat16)
+    loads[7].wait()
+    loads[8].wait()
     shifted = tangent.astype(jnp.float32) + dot(mixed, wo_ref[...])
     square = jnp.mean(shifted * shifted, axis=-1, keepdims=True)
     normed = shifted * (1.0 / jnp.sqrt(square + 1e-06)) * gain_ref[...]
@@ -250,19 +281,25 @@
     width = points.shape[1]
     n_slots = tile_slots.shape[-1]
     vmem = pl.BlockSpec(memory_space=pltpu.VMEM)
-    smem = pl.BlockSpec(memory_space=pltpu.SMEM)
     dma = pltpu.SemaphoreType.DMA
     return pl.pallas_call(
         functools.partial(kernel, n_dst, n_src, tile, n_slots),
         out_shape=jax.ShapeDtypeStruct((tile, width), jnp.bfloat16),
-        in_specs=[vmem] * 6 + [smem, smem, pl.BlockSpec(memory_space=pl.ANY)],
+        in_specs=[pl.BlockSpec(memory_space=pltpu.HBM)] * 9,
         out_specs=vmem,
         scratch_shapes=[
+            pltpu.VMEM((tile, width), jnp.bfloat16),
+            *[pltpu.VMEM((width, width), jnp.bfloat16)] * 4,
+            pltpu.VMEM((1, width), jnp.float32),
+            pltpu.SMEM((1, 1), jnp.int32),
+            pltpu.SMEM((1, 1, n_slots), jnp.int32),
+            pltpu.VMEM((1, 1, n_slots, tile, tile), jnp.int32),
             pltpu.VMEM((n_dst, tile, width), jnp.bfloat16),
             pltpu.VMEM((n_src, tile, width), jnp.bfloat16),
-            pltpu.VMEM((n_slots, tile, tile), jnp.int32),
             pltpu.VMEM((n_slots + 1, tile, tile), jnp.float32),
             pltpu.SMEM((n_src * n_dst,), jnp.int32),
+            pltpu.VMEM((width, width), jnp.bfloat16),
+            pltpu.VMEM((HEADS * tile, width), jnp.bfloat16),
             pltpu.VMEM((n_dst * tile, width), jnp.bfloat16),
             pltpu.VMEM((width, n_dst * tile), jnp.bfloat16),
             pltpu.VMEM((n_dst * tile, HEADS * tile), jnp.float32),
@@ -271,17 +308,17 @@
             pltpu.VMEM((n_src, 2 * HEADS, tile), jnp.float32),
             pltpu.VMEM((n_src, width, tile), jnp.bfloat16),
             pltpu.VMEM((n_src, 2 * HEADS, tile), jnp.float32),
-            dma,
+            dma((9,)),
             dma((n_dst,)), dma((n_dst,)),
             dma((n_src,)), dma((n_src,)),
             dma((n_src,)), dma((n_src,)),
             dma((n_src,)), dma((n_src,)),
         ],
         compiler_params=pltpu.CompilerParams(
-            collective_id=0, has_side_effects=True, vmem_limit_bytes=44 * 1024 * 1024),
+            collective_id=0, has_side_effects=True, vmem_limit_bytes=58 * 1024 * 1024),
     )(
         points, w_query, w_key, w_value, w_out, gain.reshape(1, width),
-        cell_counts.reshape(1), tile_slots.reshape(n_slots), edge_masks.reshape(n_slots, tile, tile),
+        cell_counts, tile_slots, edge_masks,
     )
 
 

time: 33 us -> 27.4 us (0.83)
  local copies, waits for them, and re-layouts: 6.98 us -> 1.47 us
    unnamed x17 -> x1, local copies, waits for them, and re-layouts: 6.98 us -> 1.47 us
where the time goes in v2:
time: 27.4 us; the launch traced here: 27.3 us
  Pallas kernels  25.1 us (92%)
  local copies, waits for them, and re-layouts  1.47 us (5%)
  between operations  0.66 us (2%)
    pallas_call x1, Pallas kernels, per_device(): pl.pallas_call(functools.partial(kernel, n_dst, n_src, tile, n_slots), ou...  25.1 us
    unnamed x1, local copies, waits for them, and re-layouts  1.47 us

profile of v2, /device:TPU:0, one launch (start us, length us, event | category | flops | bytes accessed | tf_op | source)
XLA Modules:
  0.0 27.3 jit_solution(6744985976708338021)
XLA Ops:
  0.7 25.1 %shard_map.91 = bf16[128,256]{1,0:T(8,128)(2,1)} custom-call(bf16[128,256]{1,0:T(8,128)(2,1)} %points_hbm.1, bf16[256,256]{1,0:T(8,128)(2,1)} %wq_hbm.1, bf16[256,256]{1,0:T(8,128)(2,1)} %wk_hbm.1, bf16[256,256]{1,0:T(8,128)(2,1)} %wv_hbm.1, bf16[256,256]{1,0:T(8,128)(2,1)} %wo_hbm.1, f32[1,256]{1,0:T(1,128)} %bitcast.1, s32[1,1]{1,0:T(1,128)S(6)} %copy.11.counts_hbm, ...), custom_call_target="tpu_custom_call" | custom-call | tf_op jit(solution)/shard_map/pallas_call | solution.py:285
  25.8 1.5 %copy.12 = bf16[128,256]{1,0:T(8,128)(2,1)} copy(bf16[128,256]{1,0:T(8,128)(2,1)} %shard_map.91) | data formatting | bytes 131072

commit v3 on v2

--- a/solution.py
+++ b/solution.py
@@ -42,7 +42,7 @@
     points_hbm, wq_hbm, wk_hbm, wv_hbm, wo_hbm, gain_hbm, counts_hbm, slots_hbm, masks_hbm,
     out_ref,
     points_ref, wq_ref, wk_ref, wv_ref, wo_ref, gain_ref, counts_ref, slots_ref, masks,
-    kt, qt, bias, inv, wv_turned, q_heads, k_all, v_all, scores, probs, acc_out, stat_out, acc_in, stat_in,
+    kt, qt, bias, inv, wv_turned, q_heads, k_all, v_all, scores, probs, tops, row_tops, sums, acc_out, stat_out, acc_in, stat_in,
     load_sem, kt_send, kt_recv, qt_send, qt_recv, acc_send, acc_recv, stat_send, stat_recv,
 ):
     d = lax.axis_index("dst")
@@ -128,7 +128,9 @@
     loads[5].wait()
 
     loads[6].wait()
-    bias[n_slots] = jnp.full((tile, tile), NEG, jnp.float32)
+    tops[:, n_slots] = jnp.full((HEADS // 2, 8, 2 * tile), NEG, jnp.float32)
+    sums[:, n_slots] = jnp.zeros((HEADS // 2, 8, 2 * tile), jnp.float32)
+    probs[:, n_slots] = jnp.zeros((HEADS // 2, tile, 2 * tile), jnp.bfloat16)
 
     def turn_masks(step, carry):
         for member in range(8):
@@ -141,7 +143,7 @@
     def project_slot(slot):
         rows = kt[slot]
         at = pl.ds(pl.multiple_of(slot * tile, tile), tile)
-        k_all[at, :] = dot(rows, wk_ref[...]).astype(jnp.bfloat16)
+        k_all[slot] = dot(rows, wk_ref[...]).astype(jnp.bfloat16)
         v_all[:, at] = dot(wv_turned[...], rows, ((1,), (1,))).astype(jnp.bfloat16)
 
     own_v = dot(wv_turned[...], tangent, ((1,), (1,))).astype(jnp.bfloat16).astype(jnp.float32)
@@ -155,108 +157,140 @@
 
     lax.fori_loop(1, n_dst, take_keys, 0)
 
-    group = min(8, n_dst)
-
-    def over_groups(body, start):
-        if n_dst == group:
-            return body(0, start)
-        return lax.fori_loop(0, n_dst // group, body, start)
-
-    def attend(r):
+    group = min(16, n_slots)
+    pairs = HEADS // 2
+
+    def over_slots(body):
+        if n_slots == group:
+            for t in range(n_slots):
+                body(t)
+            return
+
+        def some(g, carry):
+            for member in range(group):
+                body(g * group + member)
+            return carry
+
+        lax.fori_loop(0, n_slots // group, some, 0)
+
+    def project_queries(r):
         q = (dot(qt[r], wq_ref[...]).astype(jnp.bfloat16).astype(jnp.float32) * scale).astype(jnp.bfloat16)
         for h in range(HEADS):
-            q_heads[h * tile:(h + 1) * tile, h * head:(h + 1) * head] = q[:, h * head:(h + 1) * head]
-
-        def score_group(g, tops):
-            tops = list(tops)
-            for member in range(group):
-                k = g * group + member
-                at = pl.ds(k * tile, tile) if isinstance(k, int) else pl.ds(pl.multiple_of(k * tile, tile), tile)
-                prod = dot(k_all[at, :], q_heads[...], ((1,), (1,)))
-                term = bias[inv[r * n_dst + k]]
-                for h in range(HEADS):
-                    part = prod[:, h * tile:(h + 1) * tile] + term
-                    scores[at, h * tile:(h + 1) * tile] = part
-                    tops[h] = jnp.maximum(tops[h], jnp.max(fold_rows(part), axis=0))
-            return tuple(tops)
-
-        tops = over_groups(score_group, tuple(jnp.full((8, tile), NEG, jnp.float32) for _ in range(HEADS)))
-        tops = [jnp.max(t, axis=0, keepdims=True) for t in tops]
-
-        def exp_group(g, sums):
-            sums = list(sums)
-            for member in range(group):
-                k = g * group + member
-                at = pl.ds(k * tile, tile) if isinstance(k, int) else pl.ds(pl.multiple_of(k * tile, tile), tile)
-                for h in range(HEADS):
-                    lanes = slice(h * tile, (h + 1) * tile)
-                    p = jnp.exp(scores[at, lanes] - tops[h])
-                    sums[h] = sums[h] + jnp.sum(fold_rows(p), axis=0)
-                    probs[at, lanes] = p.astype(jnp.bfloat16)
-            return tuple(sums)
-
-        sums = over_groups(exp_group, tuple(jnp.zeros((8, tile), jnp.float32) for _ in range(HEADS)))
-        sums = [jnp.sum(t, axis=0, keepdims=True) for t in sums]
-        accs = []
-        for j in range(HEADS // 2):
-            both = dot(v_all[2 * j * head:2 * (j + 1) * head, :], probs[:, 2 * j * tile:2 * (j + 1) * tile])
-            accs.append(both[:head, :tile])
-            accs.append(both[head:, tile:])
-        return tops, sums, accs
-
-    def acc_copy(slot, peer):
+            half = h % 2
+            q_heads[r, h // 2, half * tile:(half + 1) * tile, half * head:(half + 1) * head] = (
+                q[:, h * head:(h + 1) * head])
+
+    def attend(j):
+        lanes = slice(2 * j * head, 2 * (j + 1) * head)
+
+        def score(t):
+            cell = slots_ref[0, 0, t]
+            r = lax.div(cell, jnp.int32(n_dst))
+            k = lax.rem(cell, jnp.int32(n_dst))
+            prod = dot(k_all[k, :, lanes], q_heads[r, j], ((1,), (1,)))
+            term = bias[t]
+            for half in range(2):
+                at = slice(half * tile, (half + 1) * tile)
+                part = prod[:, at] + term
+                scores[j, t, :, at] = part
+                tops[j, t, :, at] = jnp.max(fold_rows(part), axis=0)
+
+        over_slots(score)
+        for r in range(n_src):
+            top = tops[j, inv[r * n_dst]]
+            for k in range(1, n_dst):
+                top = jnp.maximum(top, tops[j, inv[r * n_dst + k]])
+            row_tops[j, r] = jnp.broadcast_to(jnp.max(top, axis=0, keepdims=True), top.shape)
+
+        def weigh(t):
+            r = lax.div(slots_ref[0, 0, t], jnp.int32(n_dst))
+            for half in range(2):
+                at = slice(half * tile, (half + 1) * tile)
+                p = jnp.exp(fold_rows(scores[j, t, :, at]) - row_tops[j, r, :, at][None])
+                sums[j, t, :, at] = jnp.sum(p, axis=0)
+                probs[j, t, :, at] = p.reshape(tile, tile).astype(jnp.bfloat16)
+
+        over_slots(weigh)
+
+    def collect(j, r):
+        listing = [inv[r * n_dst + k] for k in range(n_dst)]
+        total = sums[j, listing[0]]
+        for t in listing[1:]:
+            total = total + sums[j, t]
+        total = jnp.sum(total, axis=0, keepdims=True)
+        top = row_tops[j, r][:1]
+        both = dot(v_all[2 * j * head:2 * (j + 1) * head, :],
+                   jnp.concatenate([probs[j, t] for t in listing], axis=0))
+        return (
+            [top[:, :tile], top[:, tile:]],
+            [total[:, :tile], total[:, tile:]],
+            [both[:head, :tile], both[head:, tile:]],
+        )
+
+    def acc_copy(j, slot, peer):
         return pltpu.make_async_remote_copy(
-            src_ref=acc_out.at[peer], dst_ref=acc_in.at[slot],
-            send_sem=acc_send.at[peer], recv_sem=acc_recv.at[slot],
+            src_ref=acc_out.at[j, peer], dst_ref=acc_in.at[j, slot],
+            send_sem=acc_send.at[j, peer], recv_sem=acc_recv.at[j, slot],
             device_id=(d, peer), device_id_type=MESH)
 
-    def stat_copy(slot, peer):
+    def stat_copy(j, slot, peer):
         return pltpu.make_async_remote_copy(
-            src_ref=stat_out.at[peer], dst_ref=stat_in.at[slot],
-            send_sem=stat_send.at[peer], recv_sem=stat_recv.at[slot],
+            src_ref=stat_out.at[j, peer], dst_ref=stat_in.at[j, slot],
+            send_sem=stat_send.at[j, peer], recv_sem=stat_recv.at[j, slot],
             device_id=(d, peer), device_id_type=MESH)
 
+    project_queries(s)
     for off in src_order:
         r = src_peer(off)
         q_copy(r, r).wait_recv()
-        tops, sums, accs = attend(r)
-        stat_out[r] = jnp.concatenate(tops + sums, axis=0)
-        acc_out[r] = jnp.concatenate(accs, axis=0).astype(jnp.bfloat16)
-        acc_copy(s, r).start()
-        stat_copy(s, r).start()
-
-    tops, sums, accs = attend(s)
-    own_prod = dot(k_all[pl.ds(pl.multiple_of(d * tile, tile), tile), :], q_heads[...], ((1,), (1,)))
+        project_queries(r)
+
+    own_parts = []
+    for j in range(pairs):
+        attend(j)
+        for off in src_order:
+            r = src_peer(off)
+            part_tops, part_sums, part_accs = collect(j, r)
+            stat_out[j, r] = jnp.concatenate(part_tops + part_sums + part_tops + part_sums, axis=0)
+            acc_out[j, r] = jnp.concatenate(part_accs, axis=0).astype(jnp.bfloat16)
+            acc_copy(j, s, r).start()
+            stat_copy(j, s, r).start()
+        own_parts.append(collect(j, s))
+
     diagonal = lax.broadcasted_iota(jnp.int32, (tile, tile), 0) == lax.broadcasted_iota(jnp.int32, (tile, tile), 1)
-    self_score = [
-        jnp.sum(jnp.where(diagonal, own_prod[:, h * tile:(h + 1) * tile], 0.0), axis=0, keepdims=True)
-        for h in range(HEADS)
-    ]
-    parts = [(tops, sums, accs)]
+    self_score = []
+    parts = [tuple(sum((own_parts[j][n] for j in range(pairs)), []) for n in range(3))]
+    for j in range(pairs):
+        own_prod = dot(k_all[d, :, 2 * j * head:2 * (j + 1) * head], q_heads[s, j], ((1,), (1,)))
+        for half in range(2):
+            self_score.append(jnp.sum(
+                jnp.where(diagonal, own_prod[:, half * tile:(half + 1) * tile], 0.0), axis=0, keepdims=True))
     for off in src_order:
         c = src_peer(off)
-        acc_copy(c, c).wait_recv()
-        stat_copy(c, c).wait_recv()
-        stat = stat_in[c]
-        acc = acc_in[c].astype(jnp.float32)
-        parts.append((
-            [stat[h:h + 1] for h in range(HEADS)],
-            [stat[HEADS + h:HEADS + h + 1] for h in range(HEADS)],
-            [acc[h * head:(h + 1) * head] for h in range(HEADS)],
-        ))
+        got = ([], [], [])
+        for j in range(pairs):
+            acc_copy(j, c, c).wait_recv()
+            stat_copy(j, c, c).wait_recv()
+            stat = stat_in[j, c]
+            acc = acc_in[j, c].astype(jnp.float32)
+            for half in range(2):
+                got[0].append(stat[half:half + 1])
+                got[1].append(stat[2 + half:3 + half])
+                got[2].append(acc[half * head:(half + 1) * head])
+        parts.append(got)
 
     mixed = []
     for h in range(HEADS):
         top = self_score[h]
-        for tops, _, _ in parts:
-            top = jnp.maximum(top, tops[h])
+        for part in parts:
+            top = jnp.maximum(top, part[0][h])
         weight = jnp.exp(self_score[h] - top)
         total = weight
         number = weight.astype(jnp.bfloat16).astype(jnp.float32) * own_v[h * head:(h + 1) * head]
-        for tops, sums, accs in parts:
-            factor = jnp.exp(tops[h] - top)
-            total = total + sums[h] * factor
-            number = number + accs[h] * factor
+        for part_tops, part_sums, part_accs in parts:
+            factor = jnp.exp(part_tops[h] - top)
+            total = total + part_sums[h] * factor
+            number = number + part_accs[h] * factor
         mixed.append(number / total)
     mixed = turned(jnp.concatenate(mixed, axis=0).astype(jnp.bfloat16), eye_tile).astype(jnp.bfloat16)
     loads[7].wait()
@@ -272,14 +306,16 @@
     for off in src_order:
         r = src_peer(off)
         q_copy(s, r).wait_send()
-        acc_copy(s, r).wait_send()
-        stat_copy(s, r).wait_send()
+        for j in range(pairs):
+            acc_copy(j, s, r).wait_send()
+            stat_copy(j, s, r).wait_send()
 
 
 def per_device(n_dst, n_src, points, w_query, w_key, w_value, w_out, gain, cell_counts, tile_slots, edge_masks):
     tile = points.shape[0]
     width = points.shape[1]
     n_slots = tile_slots.shape[-1]
+    pairs = HEADS // 2
     vmem = pl.BlockSpec(memory_space=pltpu.VMEM)
     dma = pltpu.SemaphoreType.DMA
     return pl.pallas_call(
@@ -296,23 +332,26 @@
             pltpu.VMEM((1, 1, n_slots, tile, tile), jnp.int32),
             pltpu.VMEM((n_dst, tile, width), jnp.bfloat16),
             pltpu.VMEM((n_src, tile, width), jnp.bfloat16),
-            pltpu.VMEM((n_slots + 1, tile, tile), jnp.float32),
+            pltpu.VMEM((n_slots, tile, tile), jnp.float32),
             pltpu.SMEM((n_src * n_dst,), jnp.int32),
             pltpu.VMEM((width, width), jnp.bfloat16),
-            pltpu.VMEM((HEADS * tile, width), jnp.bfloat16),
-            pltpu.VMEM((n_dst * tile, width), jnp.bfloat16),
+            pltpu.VMEM((n_src, pairs, 2 * tile, width // pairs), jnp.bfloat16),
+            pltpu.VMEM((n_dst, tile, width), jnp.bfloat16),
             pltpu.VMEM((width, n_dst * tile), jnp.bfloat16),
-            pltpu.VMEM((n_dst * tile, HEADS * tile), jnp.float32),
-            pltpu.VMEM((n_dst * tile, HEADS * tile), jnp.bfloat16),
-            pltpu.VMEM((n_src, width, tile), jnp.bfloat16),
-            pltpu.VMEM((n_src, 2 * HEADS, tile), jnp.float32),
-            pltpu.VMEM((n_src, width, tile), jnp.bfloat16),
-            pltpu.VMEM((n_src, 2 * HEADS, tile), jnp.float32),
+            pltpu.VMEM((pairs, n_slots, tile, 2 * tile), jnp.float32),
+            pltpu.VMEM((pairs, n_slots + 1, tile, 2 * tile), jnp.bfloat16),
+            pltpu.VMEM((pairs, n_slots + 1, 8, 2 * tile), jnp.float32),
+            pltpu.VMEM((pairs, n_src, 8, 2 * tile), jnp.float32),
+            pltpu.VMEM((pairs, n_slots + 1, 8, 2 * tile), jnp.float32),
+            pltpu.VMEM((pairs, n_src, width // pairs, tile), jnp.bfloat16),
+            pltpu.VMEM((pairs, n_src, 8, tile), jnp.float32),
+            pltpu.VMEM((pairs, n_src, width // pairs, tile), jnp.bfloat16),
+            pltpu.VMEM((pairs, n_src, 8, tile), jnp.float32),
             dma((9,)),
             dma((n_dst,)), dma((n_dst,)),
             dma((n_src,)), dma((n_src,)),
-            dma((n_src,)), dma((n_src,)),
-            dma((n_src,)), dma((n_src,)),
+            dma((pairs, n_src)), dma((pairs, n_src)),
+            dma((pairs, n_src)), dma((pairs, n_src)),
         ],
         compiler_params=pltpu.CompilerParams(
             collective_id=0, has_side_effects=True, vmem_limit_bytes=58 * 1024 * 1024),

time: 27.4 us -> 27.2 us (level)
  no operation moved by 1% of the time
where the time goes in v3:
time: 27.2 us; the launch traced here: 27 us
  Pallas kernels  24.9 us (92%)
  local copies, waits for them, and re-layouts  1.47 us (5%)
  between operations  0.66 us (2%)
    pallas_call x1, Pallas kernels, per_device(): pl.pallas_call(functools.partial(kernel, n_dst, n_src, tile, n_slots), ou...  24.9 us
    unnamed x1, local copies, waits for them, and re-layouts  1.47 us

profile of v3, /device:TPU:0, one launch (start us, length us, event | category | flops | bytes accessed | tf_op | source)
XLA Modules:
  0.0 27.0 jit_solution(8760077346449579711)
XLA Ops:
  0.7 24.9 %shard_map.91 = bf16[128,256]{1,0:T(8,128)(2,1)} custom-call(bf16[128,256]{1,0:T(8,128)(2,1)} %points_hbm.1, bf16[256,256]{1,0:T(8,128)(2,1)} %wq_hbm.1, bf16[256,256]{1,0:T(8,128)(2,1)} %wk_hbm.1, bf16[256,256]{1,0:T(8,128)(2,1)} %wv_hbm.1, bf16[256,256]{1,0:T(8,128)(2,1)} %wo_hbm.1, f32[1,256]{1,0:T(1,128)} %bitcast.1, s32[1,1]{1,0:T(1,128)S(6)} %copy.11.counts_hbm, ...), custom_call_target="tpu_custom_call" | custom-call | tf_op jit(solution)/shard_map/pallas_call | solution.py:321
  25.6 1.5 %copy.12 = bf16[128,256]{1,0:T(8,128)(2,1)} copy(bf16[128,256]{1,0:T(8,128)(2,1)} %shard_map.91) | data formatting | bytes 131072

commit v4 on v3

--- a/solution.py
+++ b/solution.py
@@ -43,7 +43,7 @@
     out_ref,
     points_ref, wq_ref, wk_ref, wv_ref, wo_ref, gain_ref, counts_ref, slots_ref, masks,
     kt, qt, bias, inv, wv_turned, q_heads, k_all, v_all, scores, probs, tops, row_tops, sums, acc_out, stat_out, acc_in, stat_in,
-    load_sem, kt_send, kt_recv, qt_send, qt_recv, acc_send, acc_recv, stat_send, stat_recv,
+    load_sem, kt_send, kt_pass, kt_recv, qt_send, qt_recv, acc_send, acc_recv, stat_send, stat_recv,
 ):
     d = lax.axis_index("dst")
     s = lax.axis_index("src")
@@ -60,8 +60,10 @@
     barrier = pltpu.get_barrier_semaphore()
     for off in range(1, n_src):
         pl.semaphore_signal(barrier, inc=1, device_id=(d, src_peer(off)), device_id_type=MESH)
-    for off in range(1, n_dst):
-        pl.semaphore_signal(barrier, inc=1, device_id=(dst_peer(off), s), device_id_type=MESH)
+    twin = d + 1 - 2 * lax.rem(d, 2)
+    k_peers = [dst_peer(off) for off in range(2, n_dst, 2)] + [twin]
+    for peer in k_peers:
+        pl.semaphore_signal(barrier, inc=1, device_id=(peer, s), device_id_type=MESH)
 
     loads = [
         pltpu.make_async_copy(source, target, load_sem.at[index])
@@ -77,7 +79,7 @@
     tangent = log_map(points_ref[...])
     kt[d] = tangent
     qt[s] = tangent
-    pl.semaphore_wait(barrier, n_src - 1 + n_dst - 1)
+    pl.semaphore_wait(barrier, n_src - 1 + n_dst // 2)
 
     def q_copy(slot, peer):
         return pltpu.make_async_remote_copy(
@@ -91,11 +93,17 @@
             send_sem=kt_send.at[peer], recv_sem=kt_recv.at[slot],
             device_id=(peer, s), device_id_type=MESH)
 
+    def k_pass(slot):
+        return pltpu.make_async_remote_copy(
+            src_ref=kt.at[slot], dst_ref=kt.at[slot],
+            send_sem=kt_pass.at[slot], recv_sem=kt_recv.at[slot],
+            device_id=(twin, s), device_id_type=MESH)
+
     src_order = [2, 1, 3] if n_src == 4 else list(range(1, n_src))
     for off in src_order:
         q_copy(s, src_peer(off)).start()
-    for off in range(1, n_dst):
-        k_copy(d, dst_peer(off)).start()
+    for peer in k_peers:
+        k_copy(d, peer).start()
 
     loads[1].wait()
     loads[2].wait()
@@ -127,6 +135,27 @@
     loads[4].wait()
     loads[5].wait()
 
+    def project_slot(slot):
+        rows = kt[slot]
+        at = pl.ds(pl.multiple_of(slot * tile, tile), tile)
+        k_all[slot] = dot(rows, wk_ref[...]).astype(jnp.bfloat16)
+        v_all[:, at] = dot(wv_turned[...], rows, ((1,), (1,))).astype(jnp.bfloat16)
+
+    own_v = dot(wv_turned[...], tangent, ((1,), (1,))).astype(jnp.bfloat16).astype(jnp.float32)
+    project_slot(d)
+
+    k_copy(twin, twin).wait_recv()
+    project_slot(twin)
+
+    def pass_keys(half, carry):
+        slot = dst_peer(2 * half)
+        k_copy(slot, slot).wait_recv()
+        k_pass(slot).start()
+        project_slot(slot)
+        return carry
+
+    lax.fori_loop(1, n_dst // 2, pass_keys, 0)
+
     loads[6].wait()
     tops[:, n_slots] = jnp.full((HEADS // 2, 8, 2 * tile), NEG, jnp.float32)
     sums[:, n_slots] = jnp.zeros((HEADS // 2, 8, 2 * tile), jnp.float32)
@@ -140,22 +169,13 @@
 
     lax.fori_loop(0, n_slots // 8, turn_masks, 0)
 
-    def project_slot(slot):
-        rows = kt[slot]
-        at = pl.ds(pl.multiple_of(slot * tile, tile), tile)
-        k_all[slot] = dot(rows, wk_ref[...]).astype(jnp.bfloat16)
-        v_all[:, at] = dot(wv_turned[...], rows, ((1,), (1,))).astype(jnp.bfloat16)
-
-    own_v = dot(wv_turned[...], tangent, ((1,), (1,))).astype(jnp.bfloat16).astype(jnp.float32)
-    project_slot(d)
-
-    def take_keys(off, carry):
-        slot = dst_peer(off)
+    def take_keys(half, carry):
+        slot = lax.rem(twin + 2 * half, n_dst)
         k_copy(slot, slot).wait_recv()
         project_slot(slot)
         return carry
 
-    lax.fori_loop(1, n_dst, take_keys, 0)
+    lax.fori_loop(1, n_dst // 2, take_keys, 0)
 
     group = min(16, n_slots)
     pairs = HEADS // 2
@@ -301,8 +321,10 @@
     radius = jnp.sqrt(jnp.sum(normed * normed, axis=-1, keepdims=True) + 1e-06)
     out_ref[...] = (normed * sinh_over(radius * (1.0 / math.sqrt(width)))).astype(jnp.bfloat16)
 
-    for off in range(1, n_dst):
-        k_copy(d, dst_peer(off)).wait_send()
+    for peer in k_peers:
+        k_copy(d, peer).wait_send()
+    for half in range(1, n_dst // 2):
+        k_pass(dst_peer(2 * half)).wait_send()
     for off in src_order:
         r = src_peer(off)
         q_copy(s, r).wait_send()
@@ -348,7 +370,7 @@
             pltpu.VMEM((pairs, n_src, width // pairs, tile), jnp.bfloat16),
             pltpu.VMEM((pairs, n_src, 8, tile), jnp.float32),
             dma((9,)),
-            dma((n_dst,)), dma((n_dst,)),
+            dma((n_dst,)), dma((n_dst,)), dma((n_dst,)),
             dma((n_src,)), dma((n_src,)),
             dma((pairs, n_src)), dma((pairs, n_src)),
             dma((pairs, n_src)), dma((pairs, n_src)),

time: 27.2 us -> 25.5 us (0.938)
  Pallas kernels: 24.9 us -> 23.2 us
    pallas_call x1, Pallas kernels: 24.9 us -> 23.2 us  [per_device(): pl.pallas_call(functools.partial(kernel, n_dst, n_src, tile, n_slots), ou...]
where the time goes in v4:
time: 25.5 us; the launch traced here: 25.3 us
  Pallas kernels  23.2 us (91%)
  local copies, waits for them, and re-layouts  1.47 us (6%)
  between operations  0.66 us (3%)
    pallas_call x1, Pallas kernels, per_device(): pl.pallas_call(functools.partial(kernel, n_dst, n_src, tile, n_slots), ou...  23.2 us
    unnamed x1, local copies, waits for them, and re-layouts  1.47 us

profile of v4, /device:TPU:0, one launch (start us, length us, event | category | flops | bytes accessed | tf_op | source)
XLA Modules:
  0.0 25.3 jit_solution(1486099315156120732)
XLA Ops:
  0.7 23.2 %shard_map.91 = bf16[128,256]{1,0:T(8,128)(2,1)} custom-call(bf16[128,256]{1,0:T(8,128)(2,1)} %points_hbm.1, bf16[256,256]{1,0:T(8,128)(2,1)} %wq_hbm.1, bf16[256,256]{1,0:T(8,128)(2,1)} %wk_hbm.1, bf16[256,256]{1,0:T(8,128)(2,1)} %wv_hbm.1, bf16[256,256]{1,0:T(8,128)(2,1)} %wo_hbm.1, f32[1,256]{1,0:T(1,128)} %bitcast.1, s32[1,1]{1,0:T(1,128)S(6)} %copy.11.counts_hbm, ...), custom_call_target="tpu_custom_call" | custom-call | tf_op jit(solution)/shard_map/pallas_call | solution.py:343
  23.8 1.5 %copy.12 = bf16[128,256]{1,0:T(8,128)(2,1)} copy(bf16[128,256]{1,0:T(8,128)(2,1)} %shard_map.91) | data formatting | bytes 131072

commit v5 on v4

--- a/solution.py
+++ b/solution.py
@@ -43,7 +43,7 @@
     out_ref,
     points_ref, wq_ref, wk_ref, wv_ref, wo_ref, gain_ref, counts_ref, slots_ref, masks,
     kt, qt, bias, inv, wv_turned, q_heads, k_all, v_all, scores, probs, tops, row_tops, sums, acc_out, stat_out, acc_in, stat_in,
-    load_sem, kt_send, kt_pass, kt_recv, qt_send, qt_recv, acc_send, acc_recv, stat_send, stat_recv,
+    load_sem, kt_send, kt_pass, kt_recv, qt_send, qt_pass, qt_recv, acc_send, acc_recv, stat_send, stat_recv,
 ):
     d = lax.axis_index("dst")
     s = lax.axis_index("src")
@@ -87,6 +87,12 @@
             send_sem=qt_send.at[peer], recv_sem=qt_recv.at[slot],
             device_id=(d, peer), device_id_type=MESH)
 
+    def q_pass(slot):
+        return pltpu.make_async_remote_copy(
+            src_ref=qt.at[slot], dst_ref=qt.at[slot],
+            send_sem=qt_pass.at[0], recv_sem=qt_recv.at[slot],
+            device_id=(d, n_src - 1 - slot), device_id_type=MESH)
+
     def k_copy(slot, peer):
         return pltpu.make_async_remote_copy(
             src_ref=kt.at[slot], dst_ref=kt.at[slot],
@@ -100,8 +106,17 @@
             device_id=(twin, s), device_id_type=MESH)
 
     src_order = [2, 1, 3] if n_src == 4 else list(range(1, n_src))
+    relayed = n_src == 4
+    at_end = jnp.logical_or(s == 0, s == n_src - 1)
+
+    def if_direct(peer, body):
+        if relayed:
+            pl.when(jnp.logical_not(jnp.logical_and(at_end, peer + s == n_src - 1)))(body)
+        else:
+            body()
+
     for off in src_order:
-        q_copy(s, src_peer(off)).start()
+        if_direct(src_peer(off), lambda: q_copy(s, src_peer(off)).start())
     for peer in k_peers:
         k_copy(d, peer).start()
 
@@ -155,6 +170,14 @@
         return carry
 
     lax.fori_loop(1, n_dst // 2, pass_keys, 0)
+
+    if relayed:
+        across = src_peer(2)
+        q_copy(across, across).wait_recv()
+
+        @pl.when(jnp.logical_not(at_end))
+        def _():
+            q_pass(across).start()
 
     loads[6].wait()
     tops[:, n_slots] = jnp.full((HEADS // 2, 8, 2 * tile), NEG, jnp.float32)
@@ -262,7 +285,8 @@
     project_queries(s)
     for off in src_order:
         r = src_peer(off)
-        q_copy(r, r).wait_recv()
+        if not (relayed and off == 2):
+            q_copy(r, r).wait_recv()
         project_queries(r)
 
     own_parts = []
@@ -321,13 +345,18 @@
     radius = jnp.sqrt(jnp.sum(normed * normed, axis=-1, keepdims=True) + 1e-06)
     out_ref[...] = (normed * sinh_over(radius * (1.0 / math.sqrt(width)))).astype(jnp.bfloat16)
 
+    if relayed:
+        @pl.when(jnp.logical_not(at_end))
+        def _():
+            q_pass(src_peer(2)).wait_send()
+
     for peer in k_peers:
         k_copy(d, peer).wait_send()
     for half in range(1, n_dst // 2):
         k_pass(dst_peer(2 * half)).wait_send()
     for off in src_order:
         r = src_peer(off)
-        q_copy(s, r).wait_send()
+        if_direct(r, lambda: q_copy(s, r).wait_send())
         for j in range(pairs):
             acc_copy(j, s, r).wait_send()
             stat_copy(j, s, r).wait_send()
@@ -371,7 +400,7 @@
             pltpu.VMEM((pairs, n_src, 8, tile), jnp.float32),
             dma((9,)),
             dma((n_dst,)), dma((n_dst,)), dma((n_dst,)),
-            dma((n_src,)), dma((n_src,)),
+            dma((n_src,)), dma((1,)), dma((n_src,)),
             dma((pairs, n_src)), dma((pairs, n_src)),
             dma((pairs, n_src)), dma((pairs, n_src)),
         ],

time: 25.5 us -> 25.4 us (level)
  no operation moved by 1% of the time
where the time goes in v5:
time: 25.4 us; the launch traced here: 25.2 us
  Pallas kernels  23 us (91%)
  local copies, waits for them, and re-layouts  1.47 us (6%)
  between operations  0.66 us (3%)
    pallas_call x1, Pallas kernels, per_device(): pl.pallas_call(functools.partial(kernel, n_dst, n_src, tile, n_slots), ou...  23 us
    unnamed x1, local copies, waits for them, and re-layouts  1.47 us

profile of v5, /device:TPU:0, one launch (start us, length us, event | category | flops | bytes accessed | tf_op | source)
XLA Modules:
  0.0 25.2 jit_solution(5123684888738980934)
XLA Ops:
  0.7 23.0 %shard_map.91 = bf16[128,256]{1,0:T(8,128)(2,1)} custom-call(bf16[128,256]{1,0:T(8,128)(2,1)} %points_hbm.1, bf16[256,256]{1,0:T(8,128)(2,1)} %wq_hbm.1, bf16[256,256]{1,0:T(8,128)(2,1)} %wk_hbm.1, bf16[256,256]{1,0:T(8,128)(2,1)} %wv_hbm.1, bf16[256,256]{1,0:T(8,128)(2,1)} %wo_hbm.1, f32[1,256]{1,0:T(1,128)} %bitcast.1, s32[1,1]{1,0:T(1,128)S(6)} %copy.11.counts_hbm, ...), custom_call_target="tpu_custom_call" | custom-call | tf_op jit(solution)/shard_map/pallas_call | solution.py:372
  23.7 1.5 %copy.12 = bf16[128,256]{1,0:T(8,128)(2,1)} copy(bf16[128,256]{1,0:T(8,128)(2,1)} %shard_map.91) | data formatting | bytes 131072
